TPU v7x, 32 devices: a whole 2x2x4 slice. The times are simulated.
32 devices in a mesh: grp: 4 (over y, x), cell: 8 (over z, core).
Axes of the slice: x: 2, y: 2, z: 4, core: 2. Of those that a mesh axis runs over, the one named last changes fastest.
Arguments:
- fields: bfloat16 [512, 32, 8192], P('grp', None, 'cell'), may hold values from -6 to 6
- scales: float32 [512, 32, 64], P('grp', None, 'cell'), may hold values from 0.25 to 4
- pod_basis: bfloat16 [8192, 64], P('cell'), may hold values from -0.0625 to 0.0625
- param_order: int32 [30], replicated, may hold values from 0 to 29, each once
Outputs:
- sobol_maps: float32 [30, 8192], P(None, 'cell')
- total_map: float32 [8192], P('cell')
Inputs may be any that keep to these rules, and one draw needn't show every extreme that they name: `param_order`: each parameter appears exactly once.
All inputs are finite; a program needn't handle non-finite values.
Results may differ from a plain program's by a relative error of at most 0.0003.
The roundings to bfloat16 on the way count: a program that leaves them out, or rounds other values in their place, can miss the bound.
Values sent between devices are 32-bit elements; how exact they have to be, the bound alone decides.
A program may use at most 128 MiB of HBM per device.

v0:
```python
import jax
import jax.numpy as jnp
from jax import lax
from jax.sharding import PartitionSpec as P


def project(piece, scale_piece, basis_piece):
    rows, slots, cells = piece.shape
    blocks = scale_piece.shape[2]
    dequant = (
        piece.astype(jnp.float32).reshape(rows, slots, blocks, cells // blocks)
        * scale_piece[..., None]
    ).astype(jnp.bfloat16)
    flat = dequant.reshape(rows * slots, cells)
    return jnp.dot(flat, basis_piece, preferred_element_type=jnp.float32).reshape(
        rows, slots, basis_piece.shape[1]
    )


def moments(coefficients):
    first = coefficients[:, 0]
    second_set = coefficients[:, 1]
    swapped = coefficients[:, 2:] - first[:, None, :]
    cross = jnp.einsum("rk,rpl->pkl", second_set, swapped, precision=lax.Precision.HIGHEST)
    squares = jnp.dot(first.T, first, precision=lax.Precision.HIGHEST) + jnp.dot(
        second_set.T, second_set, precision=lax.Precision.HIGHEST
    )
    column_sums = jnp.sum(first, axis=0) + jnp.sum(second_set, axis=0)
    return (cross, squares, column_sums)


def finish(cross, squares, column_sums, row_total, param_order, pod_basis, cell_total):
    count = param_order.shape[0]
    slot_cov = cross / row_total
    selector = (param_order[:, None] == jnp.arange(count)[None, :]).astype(jnp.float32)
    param_cov = jnp.einsum("sp,skl->pkl", selector, slot_cov, precision=lax.Precision.HIGHEST)
    average = column_sums / (2.0 * row_total)
    covariance = squares / (2.0 * row_total) - average[:, None] * average[None, :]
    stacked = jnp.concatenate([param_cov, covariance[None]], axis=0)
    phi = pod_basis.astype(jnp.float32)
    products = jnp.einsum("xk,pkl->pxl", phi, stacked, precision=lax.Precision.HIGHEST)
    all_maps = cell_total * jnp.sum(products * phi[None], axis=2)
    return (all_maps[:-1], all_maps[-1])


def on_device(fields, scales, pod_basis, param_order):
    row_count = fields.shape[0]
    group_count = lax.axis_size("grp")
    cell_devices = lax.axis_size("cell")
    row_total = float(row_count * group_count)
    cell_total = float(fields.shape[2] * cell_devices)
    partial_modes = project(fields, scales, pod_basis)
    coefficients = lax.psum(partial_modes, "cell")
    cross, squares, column_sums = moments(coefficients)
    cross, squares, column_sums = lax.psum((cross, squares, column_sums), "grp")
    return finish(cross, squares, column_sums, row_total, param_order, pod_basis, cell_total)


def solution(mesh):
    placed = (P("grp", None, "cell"), P("grp", None, "cell"), P("cell", None), P())
    return jax.shard_map(
        on_device,
        mesh=mesh,
        in_specs=placed,
        out_specs=(P(None, "cell"), P("cell")),
        check_vma=False,
    )
```

profile of v0, /device:TPU:0, one launch (start us, length us, event | category | flops | bytes accessed | tf_op | source)
XLA Modules:
  0.0 181.1 jit_solution(17713111657478609768)
XLA Ops:
  7.2 0.0 all-reduce.4.cloned.1.call-start
  7.2 2.7 %copy.6 = f32[128,32,8]{2,1,0:T(8,128)S(1)} copy(f32[128,32,8]{0,2,1:T(8,128)} %param.5) | data formatting | bytes 262144 | tf_op args[1]
  9.9 8.5 %mul.39 = f32[128,32,8,128]{3,2,1,0:T(8,128)} broadcast(f32[128,32,8]{2,1,0:T(8,128)S(1)} %copy.6), dimensions={0,1,2} | broadcast | bytes 16908288 | tf_op jit(solution)/shard_map/mul | solution.py:11
  18.4 18.0 %mul.40 = f32[128,32,1024]{2,1,0:T(8,128)} reshape(f32[128,32,8,128]{3,2,1,0:T(8,128)} %mul.39) | data formatting | bytes 33554432 | tf_op jit(solution)/shard_map/mul | solution.py:11
  36.5 10.5 %fusion = f32[128,32,64]{2,1,0:T(8,128)S(1)} fusion(f32[128,32,1024]{2,1,0:T(8,128)} %mul.40, bf16[128,32,1024]{2,1,0:T(8,128)(2,1)} %param.4, bf16[1024,64]{0,1:T(8,128)(2,1)S(1)} %copy-done), kind=kOutput, calls=%fused_computation.1 | convolution fusion | flops 549453824 | bytes 26345472 | tf_op jit(solution)/shard_map/dot_general | solution.py:15
  47.0 2.3 %copy.10 = f32[128,32,64]{0,2,1:T(8,128)} copy(f32[128,32,64]{2,1,0:T(8,128)S(1)} %fusion) | data formatting | bytes 2097152 | tf_op jit(solution)/shard_map/dot_general | solution.py:15
  49.3 0.0 all-reduce.4.cloned.1.call-update
  49.3 0.0 all-reduce.6.cloned.1.call-start
  49.4 61.6 %all-reduce.4.cloned.1.call-done = f32[128,32,64]{0,2,1:T(8,128)} async-done(((f32[128,32,64]{0,2,1:T(8,128)}), f32[128,32,64]{0,2,1:T(8,128)}) %all-reduce.4.cloned.1.call-update) | async-done | bytes 1048592 | tf_op jit(solution)/shard_map/psum | solution.py:53
  111.0 0.9 slice_reduce_fusion.1
  111.9 3.1 %convolution_bitcast_fusion = f32[30,64,64]{1,2,0:T(8,128)} fusion(f32[128,32,64]{0,2,1:T(8,128)} %all-reduce.4.cloned.1.call-done, f32[128,64]{0,1:T(8,128)S(1)} %get-tuple-element.6), kind=kOutput, calls=%fused_computation.4 | convolution fusion | flops 188989440 | bytes 1540096 | tf_op jit(solution)/shard_map/rk,rpl->pkl/dot_general | solution.py:24
  115.0 1.0 fusion.17
  116.0 1.0 convolution_add_fusion
  117.0 17.3 %all-reduce = (f32[64,64]{1,0:T(8,128)S(1)}, f32[64]{0:T(128)S(1)}) all-reduce(f32[64,64]{1,0:T(8,128)S(1)} %convolution_add_fusion, f32[64]{0:T(128)S(1)} %add.15), channel_id=1, replica_groups=mesh['grp'=4,'cell'=8] {'grp'}, use_global_device_ids=true, to_apply=%region_2.0 | all-reduce | flops 4160 | bytes 33280 | tf_op jit(solution)/shard_map/psum | solution.py:55
  134.3 0.1 subtract_bitcast_fusion
  134.4 0.1 copy.8
  134.5 31.9 %all-reduce.6.cloned.1.call-done = f32[30,64,64]{1,2,0:T(8,128)} async-done(((f32[30,64,64]{1,2,0:T(8,128)}), f32[30,64,64]{1,2,0:T(8,128)}) %all-reduce.6.cloned.1.call-update) | async-done | bytes 491536 | tf_op jit(solution)/shard_map/psum | solution.py:55
  166.4 1.3 broadcast_multiply_fusion
  167.7 0.9 copy.11
  168.6 0.7 fusion.13
  169.3 0.6 copy.12
  169.9 3.7 %fusion.1 = f32[31,1024]{1,0:T(8,128)S(1)} fusion(f32[1024,64]{0,1:T(8,128)S(1)} %convert_element_type.14, f32[1,64,64]{1,2,0:T(8,128)S(1)} %copy.8, f32[30,64,64]{1,2,0:T(8,128)S(1)} %copy.12, bf16[1024,64]{0,1:T(8,128)(2,1)S(1)} %copy-done), kind=kOutput, calls=%fused_computation.3 | convolution fusion | flops 1564439552 | bytes 1028096 | tf_op jit(solution)/shard_map/xk,pkl->pxl/dot_general | solution.py:41
  173.7 0.6 slice.24
  174.3 0.0 copy-done.1
  (10 shorter events, 0.1 us)
Async XLA Ops:
  7.2 103.8 %all-reduce.4.cloned.1.call-start = ((), (), s32[]{:S(2)}) async-start(), calls=%async_computation | async-start | bytes 2097152 | tf_op jit(solution)/shard_map/psum | solution.py:53
  18.4 18.1 %copy-start = (bf16[1024,64]{0,1:T(8,128)(2,1)S(1)}, bf16[1024,64]{0,1:T(8,128)(2,1)}, u32[]{:S(2)}) copy-start(bf16[1024,64]{0,1:T(8,128)(2,1)} %param.6) | copy-start | bytes 393220
  47.0 121.6 %copy-start.2 = (s32[30]{0:T(128)S(1)}, s32[30]{0:T(128)}, u32[]{:S(2)}) copy-start(s32[30]{0:T(128)} %param.7) | copy-start | bytes 364
  49.3 117.1 %all-reduce.6.cloned.1.call-start = ((), (), s32[]{:S(2)}) async-start(), calls=%async_computation.1 | async-start | bytes 1966080 | tf_op jit(solution)/shard_map/psum | solution.py:55
  173.6 0.7 copy-start.1
Sparse Core Ops, SparseCore 0:
  49.4 61.4 all-reduce.3
  115.1 51.2 all-reduce.5
where the time goes:
time: 182 us; the launch traced here: 181 us
  waiting for transfers between devices  93.5 us (51%)
  local copies, waits for them, and re-layouts  33.8 us (19%)
  matrix products  20 us (11%)
  blocking collectives  17.3 us (10%)
  between operations  14.2 us (8%)
  other arithmetic  2.26 us (1%)
    psum x1, waiting for transfers between devices, on_device(): coefficients = lax.psum(partial_modes, 'cell')  61.6 us
    psum x1, waiting for transfers between devices, on_device(): cross, squares, column_sums = lax.psum((cross, squares, column_sums), 'grp')  31.9 us
    mul x2, local copies, waits for them, and re-layouts, project(): piece.astype(jnp.float32).reshape(rows, slots, blocks, cells // blocks)  26.5 us
    psum x1, blocking collectives, on_device(): cross, squares, column_sums = lax.psum((cross, squares, column_sums), 'grp')  17.3 us
    dot_general x1, matrix products, project(): jnp.dot(flat, basis_piece, preferred_element_type=jnp.float32)  10.5 us
    dot_general x1, matrix products, finish(): jnp.einsum('xk,pkl->pxl', phi, stacked, precision=lax.Precision.HIGHEST)  3.72 us
  transfers between devices with their start and end apart: 2, of which 2 were waited for; matrix products, arithmetic and copies ran while one was open for 1% of the time, Pallas kernels for 0%

commit v1 on v0

v1 whole, which is shorter than its diff:
```python
import functools

import jax
import jax.numpy as jnp
from jax import lax
from jax.experimental import pallas as pl
from jax.experimental.pallas import tpu as pltpu
from jax.sharding import PartitionSpec as P

MESH = pl.DeviceIdType.MESH
F32, BF16 = jnp.float32, jnp.bfloat16
LANES = 128
STEP = 8


def loop(count, body):
    if count <= 8:
        for i in range(count):
            body(i)
    else:
        pl.loop(0, count)(body)


def split(x, axis):
    high = x.astype(BF16)
    low = (x - high.astype(F32)).astype(BF16)
    return jnp.concatenate([high, low], axis=axis)


def dot(a, b):
    return jnp.dot(a, b, preferred_element_type=F32)


def kernel(
    groups, cells_n, row_total, cell_total,
    fields_ref, scale_ref, basis_ref, order_ref, out_ref,
    field_buf, scale_buf, weight_buf, coef,
    ab_part, ab_recv, ab_full,
    moment, grp_recv, quarter, cell_recv, cov_full, map_recv,
    field_sem, ab_send, ab_sem, abf_send, abf_sem,
    grp_send, grp_sem, cov_send, cov_sem, covf_send, covf_sem, map_send, map_sem,
):
    rows = field_buf.shape[1]
    half = field_buf.shape[2]
    blocks = scale_ref.shape[1]
    modes = basis_ref.shape[0]
    steps = rows // STEP
    gme = lax.axis_index("grp")
    cme = lax.axis_index("cell")

    barrier = pltpu.get_barrier_semaphore()

    def greet_cell(c):
        @pl.when(c != cme)
        def _():
            pl.semaphore_signal(barrier, inc=1, device_id={"cell": c}, device_id_type=MESH)

    def greet_grp(g):
        @pl.when(g != gme)
        def _():
            pl.semaphore_signal(barrier, inc=1, device_id={"grp": g}, device_id_type=MESH)

    def field_copy(h, i):
        row = pl.multiple_of(i * STEP, STEP)
        return pltpu.make_async_copy(
            fields_ref.at[pl.ds(row, STEP), pl.ds(h * half, half), :],
            field_buf.at[h, pl.ds(row, STEP)],
            field_sem.at[h, i],
        )

    for h in range(2):
        pl.loop(0, steps)(lambda i, h=h: field_copy(h, i).start())
    loop(cells_n, greet_cell)
    loop(groups, greet_grp)

    phi_t = basis_ref[...]
    phi = phi_t.astype(F32)
    empty = jnp.zeros_like(phi)
    weight_buf[0] = jnp.concatenate([phi, empty], axis=0).T.astype(BF16)
    weight_buf[1] = jnp.concatenate([empty, phi], axis=0).T.astype(BF16)
    for b in range(blocks):
        scale_buf[b] = scale_ref[:, b, :]

    def project(h):
        @pl.loop(0, steps)
        def _(i):
            field_copy(h, i).wait()
            row = pl.multiple_of(i * STEP, STEP)
            turn = lax.rem(rows - row, rows)
            columns = []
            for b in range(blocks):
                scale = pltpu.roll(scale_buf[b, h * half:(h + 1) * half, :], turn, 1)
                pieces = []
                for r in range(STEP):
                    piece = field_buf[h, row + r, :, b * LANES:(b + 1) * LANES].astype(F32)
                    pieces.append((piece * scale[:, r:r + 1]).astype(BF16))
                columns.append(jnp.concatenate(pieces, axis=0))
            dequant = jnp.concatenate(columns, axis=1)
            result = dot(dequant, weight_buf[h]).reshape(STEP, half, LANES)
            if h == 0:
                coef[pl.ds(row, STEP)] = result
            else:
                coef[pl.ds(row, STEP)] += result

    project(0)

    first = coef[:, 0, :]
    second = coef[:, 1, :]
    both = first + pltpu.roll(second, modes, 1)
    owners = ab_part.shape[0]
    chunk = rows // owners
    ab_part[...] = both.reshape(owners, chunk, LANES)
    pl.semaphore_wait(barrier, cells_n - 1 + groups - 1)

    def ab_copy(owner, source):
        return pltpu.make_async_remote_copy(
            src_ref=ab_part.at[owner], dst_ref=ab_recv.at[source],
            send_sem=ab_send.at[owner], recv_sem=ab_sem.at[source],
            device_id={"cell": owner}, device_id_type=MESH,
        )

    def abf_copy(owner, target):
        return pltpu.make_async_remote_copy(
            src_ref=ab_full.at[owner], dst_ref=ab_full.at[owner],
            send_sem=abf_send.at[target], recv_sem=abf_sem.at[owner],
            device_id={"cell": target}, device_id_type=MESH,
        )

    def each(count, me, body):
        def guarded(c):
            @pl.when(c != me)
            def _():
                body(c)
        loop(count, guarded)

    each(owners, cme, lambda o: ab_copy(o, cme).start())

    def as_owner(count, body):
        if count == cells_n:
            body()
        else:
            pl.when(cme < count)(body)

    @functools.partial(as_owner, owners)
    def _():
        ab_full[cme] = ab_part[cme]

        def add(c):
            ab_copy(cme, c).wait_recv()
            ab_full[cme] += ab_recv[c]
        each(cells_n, cme, add)
        each(cells_n, cme, lambda c: abf_copy(cme, c).start())

    project(1)

    each(owners, cme, lambda o: abf_copy(o, cme).wait_recv())
    whole = ab_full[...].reshape(rows, LANES)
    whole_t = whole.T
    a_t, b_t = whole_t[:modes], whole_t[modes:]
    b_split = split(b_t, 0)
    b_left = jnp.concatenate([b_split, b_split], axis=1)
    a_split = split(a_t, 0)

    lane = lax.broadcasted_iota(jnp.int32, (rows, LANES), 1)
    part = ab_part[...].reshape(rows, LANES)
    swapped_part = pltpu.roll(part, modes, 1)
    a_twice = jnp.where(lane < modes, part, swapped_part)
    b_twice = jnp.where(lane < modes, swapped_part, part)
    a_right = jnp.where(lane < modes, 0.0, a_twice)

    sums = jnp.sum(part, axis=0, keepdims=True)
    sums = sums + pltpu.roll(sums, modes, 1)
    own_square = dot(jnp.concatenate([a_split, a_split], axis=1), split(a_twice, 0))
    own_square = own_square[:modes] + own_square[modes:]
    mode_lane = lax.broadcasted_iota(jnp.int32, (modes, LANES), 1)

    def grp_copy(target, source):
        return pltpu.make_async_remote_copy(
            src_ref=moment.at[target], dst_ref=grp_recv.at[source],
            send_sem=grp_send.at[target], recv_sem=grp_sem.at[source],
            device_id={"grp": target}, device_id_type=MESH,
        )

    pairs = half // groups
    tiles = modes // 8
    for g in range(groups):
        for p in range(0, pairs, 2):
            sides = []
            for s in (g * pairs + p, g * pairs + p + 1):
                sides.append(coef[:, s, :] - (a_right if s < 2 else a_twice))
            product = dot(b_left, split(jnp.concatenate(sides, axis=1), 0))
            product = product[:modes] + product[modes:]
            for q in range(2):
                s = g * pairs + p + q
                matrix = product[:, q * LANES:(q + 1) * LANES]
                if s == 0:
                    matrix = jnp.where(mode_lane < modes, sums, matrix)
                if s == 1:
                    matrix = jnp.where(mode_lane < modes, matrix + own_square, matrix)
                at = (p + q) * tiles
                moment[g, at:at + tiles] = matrix.reshape(tiles, 8, LANES)

        @pl.when(g != gme)
        def _():
            grp_copy(g, gme).start()

    grp_recv[gme] = moment[gme]
    each(groups, gme, lambda g: grp_copy(gme, g).wait_recv())
    total = grp_recv[0]
    for g in range(1, groups):
        total = total + grp_recv[g]
    quarter[...] = total

    cov_owners, share = cov_full.shape[0], cov_full.shape[1]

    def cov_copy(owner, source):
        return pltpu.make_async_remote_copy(
            src_ref=quarter.at[pl.ds(owner * share, share)], dst_ref=cell_recv.at[source],
            send_sem=cov_send.at[owner], recv_sem=cov_sem.at[source],
            device_id={"cell": owner}, device_id_type=MESH,
        )

    def covf_copy(owner, target):
        return pltpu.make_async_remote_copy(
            src_ref=cov_full.at[owner], dst_ref=cov_full.at[owner],
            send_sem=covf_send.at[target], recv_sem=covf_sem.at[owner],
            device_id={"cell": target}, device_id_type=MESH,
        )

    each(cov_owners, cme, lambda o: cov_copy(o, cme).start())

    @functools.partial(as_owner, cov_owners)
    def _():
        cov_full[cme] = quarter[pl.ds(cme * share, share)]

        def add(c):
            cov_copy(cme, c).wait_recv()
            cov_full[cme] += cell_recv[c]
        each(cells_n, cme, add)
        each(cells_n, cme, lambda c: covf_copy(cme, c).start())

    slots = 2 * half
    count = order_ref.shape[1]
    param = lax.broadcasted_iota(jnp.int32, (slots, count), 0)
    chosen = (order_ref[...] == param).astype(F32).astype(BF16)
    swap = lax.broadcasted_iota(jnp.int32, (count, slots), 0) + 2
    place = lax.broadcasted_iota(jnp.int32, (count, slots), 1)
    per = 2 * pairs
    stands = (lax.rem(place, per) // pairs) * half + (place // per) * pairs + lax.rem(place, pairs)
    select = dot(chosen, (stands == swap).astype(F32).astype(BF16))
    out_row = lax.broadcasted_iota(jnp.int32, (slots, slots), 0)
    in_row = lax.broadcasted_iota(jnp.int32, (slots, slots), 1)
    select = jnp.where((out_row == count) & (in_row == 1), 1.0, select).astype(BF16)
    select = jnp.concatenate([select] * 4, axis=1)
    basis_four = jnp.concatenate([phi_t] * 4, axis=0)

    each(cov_owners, cme, lambda o: covf_copy(o, cme).wait_recv())
    pair_rows = cov_full[...].reshape(pairs * modes, LANES)
    matrices = [pair_rows[p * modes:(p + 1) * modes] * (1.0 / row_total) for p in range(pairs)]
    average = matrices[0] * 0.5
    outer = average * jnp.pad(average.T[:modes], ((0, 0), (0, LANES - modes)))
    special = (mode_lane < modes) & (gme == 0)
    matrices[1] = jnp.where(special, matrices[1] * 0.5 - outer, matrices[1])
    left = jnp.concatenate(
        [jnp.where(mode_lane < modes, m, 0.0) for m in matrices]
        + [jnp.where(mode_lane < modes, 0.0, m) for m in matrices],
        axis=0,
    )
    products = dot(split(left, 1), basis_four)
    cells = products.shape[1]
    products = products.reshape(per, modes, cells) * phi[None]
    map_recv[gme] = jnp.sum(products, axis=1) * cell_total

    def map_copy(source, target):
        return pltpu.make_async_remote_copy(
            src_ref=map_recv.at[source], dst_ref=map_recv.at[source],
            send_sem=map_send.at[target], recv_sem=map_sem.at[source],
            device_id={"grp": target}, device_id_type=MESH,
        )

    each(groups, gme, lambda g: map_copy(gme, g).start())
    each(groups, gme, lambda g: map_copy(g, gme).wait_recv())
    maps = map_recv[...].reshape(slots, cells)
    high = maps.astype(BF16)
    rest = maps - high.astype(F32)
    middle = rest.astype(BF16)
    low = (rest - middle.astype(F32)).astype(BF16)
    parts = jnp.concatenate([high, middle, low, jnp.zeros_like(low)], axis=0)
    out_ref[...] = dot(select, parts)

    each(owners, cme, lambda o: ab_copy(o, cme).wait_send())
    each(groups, gme, lambda g: grp_copy(g, gme).wait_send())
    each(cov_owners, cme, lambda o: cov_copy(o, cme).wait_send())
    each(groups, gme, lambda g: map_copy(gme, g).wait_send())
    as_owner(owners, lambda: each(cells_n, cme, lambda c: abf_copy(cme, c).wait_send()))
    as_owner(cov_owners, lambda: each(cells_n, cme, lambda c: covf_copy(cme, c).wait_send()))


def on_device(fields, scales, pod_basis, param_order):
    groups = lax.axis_size("grp")
    cells_n = lax.axis_size("cell")
    rows, slots, cells = fields.shape
    blocks = scales.shape[2]
    modes = pod_basis.shape[1]
    half = slots // 2
    pairs = half // groups
    count = param_order.shape[0]
    owners = min(cells_n, rows // 8)
    tiles = pairs * modes // 8
    cov_owners = min(cells_n, tiles)
    share = tiles // cov_owners
    dma = pltpu.SemaphoreType.DMA
    vmem = pl.BlockSpec(memory_space=pltpu.VMEM)
    packed = pl.pallas_call(
        functools.partial(
            kernel, groups, cells_n, float(rows * groups), float(cells * cells_n)
        ),
        out_shape=jax.ShapeDtypeStruct((slots, cells), F32),
        in_specs=[pl.BlockSpec(memory_space=pl.ANY), vmem, vmem, vmem],
        out_specs=vmem,
        scratch_shapes=[
            pltpu.VMEM((2, rows, half, cells), BF16),
            pltpu.VMEM((blocks, slots, rows), F32),
            pltpu.VMEM((2, cells, LANES), BF16),
            pltpu.VMEM((rows, half, LANES), F32),
            pltpu.VMEM((owners, rows // owners, LANES), F32),
            pltpu.VMEM((cells_n, rows // owners, LANES), F32),
            pltpu.VMEM((owners, rows // owners, LANES), F32),
            pltpu.VMEM((groups, tiles, 8, LANES), F32),
            pltpu.VMEM((groups, tiles, 8, LANES), F32),
            pltpu.VMEM((tiles, 8, LANES), F32),
            pltpu.VMEM((cells_n, share, 8, LANES), F32),
            pltpu.VMEM((cov_owners, share, 8, LANES), F32),
            pltpu.VMEM((groups, 2 * pairs, cells), F32),
            dma((2, rows // STEP)),
            dma((owners,)), dma((cells_n,)), dma((cells_n,)), dma((owners,)),
            dma((groups,)), dma((groups,)),
            dma((cov_owners,)), dma((cells_n,)), dma((cells_n,)), dma((cov_owners,)),
            dma((groups,)), dma((groups,)),
        ],
        compiler_params=pltpu.CompilerParams(
            collective_id=0, has_side_effects=True, vmem_limit_bytes=40 * 2**20
        ),
        cost_estimate=pl.CostEstimate(
            flops=2 * rows * slots * cells * modes, bytes_accessed=2 * rows * slots * cells,
            transcendentals=0,
        ),
    )(
        fields,
        jnp.transpose(scales, (1, 2, 0)),
        jnp.transpose(pod_basis),
        param_order.reshape(1, count),
    )
    return packed[:count], packed[count]


def solution(mesh):
    placed = (P("grp", None, "cell"), P("grp", None, "cell"), P("cell", None), P())
    return jax.shard_map(
        on_device,
        mesh=mesh,
        in_specs=placed,
        out_specs=(P(None, "cell"), P("cell")),
        check_vma=False,
    )
```

time: 182 us -> 53.1 us (0.29)
  waiting for transfers between devices: 93.5 us -> 0 us
  Pallas kernels: 0 us -> 45.1 us
  local copies, waits for them, and re-layouts: 33.8 us -> 7.09 us
  matrix products: 20 us -> 0 us
  blocking collectives: 17.3 us -> 0 us
  between operations: 14.2 us -> 0.65 us
  other arithmetic: 2.26 us -> 0 us
    psum x2 -> x0, waiting for transfers between devices: 93.5 us -> none  [the longest x1 61.6 us: on_device(): coefficients = lax.psum(partial_modes, 'cell')]
    pallas_call x0 -> x1, Pallas kernels: none -> 45.1 us  [on_device(): pl.pallas_call(functools.partial(kernel, groups, cells_n, float(rows * gr...]
    mul x2 -> x0, local copies, waits for them, and re-layouts: 26.5 us -> none  [project(): piece.astype(jnp.float32).reshape(rows, slots, blocks, cells // blocks)]
    dot_general x6 -> x0, matrix products: 20 us -> none  [the longest x1 10.5 us: project(): jnp.dot(flat, basis_piece, preferred_element_type=jnp.float32)]
    psum x1 -> x0, blocking collectives: 17.3 us -> none  [on_device(): cross, squares, column_sums = lax.psum((cross, squares, column_sums), 'grp')]
    unnamed x7 -> x9, local copies, waits for them, and re-layouts: 2.76 us -> 6.49 us
    dot_general x2 -> x0, local copies, waits for them, and re-layouts: 2.91 us -> none  [the longest x1 2.32 us: project(): jnp.dot(flat, basis_piece, preferred_element_type=jnp.float32)]
  transfers between devices with their start and end apart: 2 -> 0, of which waited for: 2 -> 0; matrix products, arithmetic and copies ran while one was open for 1% -> 0% of each run, Pallas kernels for 0% -> 0%
where the time goes in v1:
time: 53.1 us; the launch traced here: 52.9 us
  Pallas kernels  45.1 us (85%)
  local copies, waits for them, and re-layouts  7.09 us (13%)
  between operations  0.65 us (1%)
    pallas_call x1, Pallas kernels, on_device(): pl.pallas_call(functools.partial(kernel, groups, cells_n, float(rows * gr...  45.1 us
    unnamed x9, local copies, waits for them, and re-layouts  6.49 us

profile of v1, /device:TPU:0, one launch (start us, length us, event | category | flops | bytes accessed | tf_op | source)
XLA Modules:
  0.0 52.9 jit_solution(391189856025093135)
XLA Ops:
  0.6 0.0 copy-start
  0.6 3.4 %copy-done = bf16[128,32,1024]{2,1,0:T(8,128)(2,1)S(1)} copy-done((bf16[128,32,1024]{2,1,0:T(8,128)(2,1)S(1)}, bf16[128,32,1024]{2,1,0:T(8,128)(2,1)}, u32[]{:S(2)}) %copy-start) | copy-done | bytes 8388632
  4.0 0.0 copy-start.1
  4.0 0.9 %copy-done.1 = f32[128,32,8]{0,2,1:T(8,128)S(1)} copy-done((f32[128,32,8]{0,2,1:T(8,128)S(1)}, f32[128,32,8]{0,2,1:T(8,128)}, u32[]{:S(2)}) %copy-start.1) | copy-done | bytes 131096
  4.9 0.0 copy-start.2
  4.9 0.9 %copy-done.2 = bf16[1024,64]{0,1:T(8,128)(2,1)S(1)} copy-done((bf16[1024,64]{0,1:T(8,128)(2,1)S(1)}, bf16[1024,64]{0,1:T(8,128)(2,1)}, u32[]{:S(2)}) %copy-start.2) | copy-done | bytes 131096
  5.8 0.0 copy-start.3
  5.8 0.7 %copy-done.3 = s32[30]{0:T(128)S(1)} copy-done((s32[30]{0:T(128)S(1)}, s32[30]{0:T(128)}, u32[]{:S(2)}) %copy-start.3) | copy-done | bytes 144
  6.5 45.1 %shard_map.59 = f32[32,1024]{1,0:T(8,128)S(1)} custom-call(bf16[128,32,1024]{2,1,0:T(8,128)(2,1)S(1)} %copy-done, f32[32,8,128]{2,1,0:T(8,128)S(1)} %bitcast.6, bf16[64,1024]{1,0:T(8,128)(2,1)S(1)} %bitcast.7, s32[1,30]{1,0:T(1,128)S(1)} %bitcast.8), custom_call_target="tpu_custom_call" | custom-call | flops 536870912 | bytes 8388608 | tf_op jit(solution)/shard_map/pallas_call | solution.py:314
  51.6 0.6 %slice.7 = f32[1,1024]{1,0:T(1,128)} slice(f32[32,1024]{1,0:T(8,128)S(1)} %shard_map.59), slice={[30:31], [0:1024]} | slice | bytes 8192 | tf_op jit(solution)/shard_map/slice | solution.py:354
  52.2 0.7 %copy.7 = f32[30,1024]{1,0:T(8,128)} copy(f32[30,1024]{1,0:T(8,128)S(1)} %bitcast.5) | data formatting | bytes 245760
Async XLA Ops:
  0.6 3.4 %copy-start = (bf16[128,32,1024]{2,1,0:T(8,128)(2,1)S(1)}, bf16[128,32,1024]{2,1,0:T(8,128)(2,1)}, u32[]{:S(2)}) copy-start(bf16[128,32,1024]{2,1,0:T(8,128)(2,1)} %fields_ref.1) | copy-start | bytes 25165828
  4.0 0.9 %copy-start.1 = (f32[128,32,8]{0,2,1:T(8,128)S(1)}, f32[128,32,8]{0,2,1:T(8,128)}, u32[]{:S(2)}) copy-start(f32[128,32,8]{0,2,1:T(8,128)} %param.5) | copy-start | bytes 393220
  4.9 0.9 %copy-start.2 = (bf16[1024,64]{0,1:T(8,128)(2,1)S(1)}, bf16[1024,64]{0,1:T(8,128)(2,1)}, u32[]{:S(2)}) copy-start(bf16[1024,64]{0,1:T(8,128)(2,1)} %param.6) | copy-start | bytes 393220
  5.8 0.7 %copy-start.3 = (s32[30]{0:T(128)S(1)}, s32[30]{0:T(128)}, u32[]{:S(2)}) copy-start(s32[30]{0:T(128)} %param.7) | copy-start | bytes 364

commit v2 on v1

--- a/solution.py
+++ b/solution.py
@@ -10,7 +10,7 @@
 MESH = pl.DeviceIdType.MESH
 F32, BF16 = jnp.float32, jnp.bfloat16
 LANES = 128
-STEP = 8
+STEP = 16
 
 
 def loop(count, body):
@@ -33,11 +33,11 @@
 
 def kernel(
     groups, cells_n, row_total, cell_total,
-    fields_ref, scale_ref, basis_ref, order_ref, out_ref,
-    field_buf, scale_buf, weight_buf, coef,
+    fields_ref, scale_any, basis_any, order_any, out_ref,
+    scale_ref, basis_ref, order_ref, field_buf, scale_buf, weight_buf, coef,
     ab_part, ab_recv, ab_full,
     moment, grp_recv, quarter, cell_recv, cov_full, map_recv,
-    field_sem, ab_send, ab_sem, abf_send, abf_sem,
+    input_sem, field_sem, ab_send, ab_sem, abf_send, abf_sem,
     grp_send, grp_sem, cov_send, cov_sem, covf_send, covf_sem, map_send, map_sem,
 ):
     rows = field_buf.shape[1]
@@ -68,21 +68,32 @@
             field_sem.at[h, i],
         )
 
+    small = [
+        pltpu.make_async_copy(source, kept, input_sem.at[n])
+        for n, (source, kept) in enumerate(
+            [(basis_any, basis_ref), (scale_any, scale_ref), (order_any, order_ref)]
+        )
+    ]
+    for copy in small:
+        copy.start()
     for h in range(2):
         pl.loop(0, steps)(lambda i, h=h: field_copy(h, i).start())
     loop(cells_n, greet_cell)
     loop(groups, greet_grp)
 
+    small[0].wait()
     phi_t = basis_ref[...]
     phi = phi_t.astype(F32)
     empty = jnp.zeros_like(phi)
     weight_buf[0] = jnp.concatenate([phi, empty], axis=0).T.astype(BF16)
     weight_buf[1] = jnp.concatenate([empty, phi], axis=0).T.astype(BF16)
+    small[1].wait()
+    small[2].wait()
     for b in range(blocks):
         scale_buf[b] = scale_ref[:, b, :]
 
-    def project(h):
-        @pl.loop(0, steps)
+    def project(h, begin, end):
+        @pl.loop(begin, end)
         def _(i):
             field_copy(h, i).wait()
             row = pl.multiple_of(i * STEP, STEP)
@@ -102,7 +113,7 @@
             else:
                 coef[pl.ds(row, STEP)] += result
 
-    project(0)
+    project(0, 0, steps)
 
     first = coef[:, 0, :]
     second = coef[:, 1, :]
@@ -141,6 +152,8 @@
         else:
             pl.when(cme < count)(body)
 
+    project(1, 0, steps // 2)
+
     @functools.partial(as_owner, owners)
     def _():
         ab_full[cme] = ab_part[cme]
@@ -151,7 +164,7 @@
         each(cells_n, cme, add)
         each(cells_n, cme, lambda c: abf_copy(cme, c).start())
 
-    project(1)
+    project(1, steps // 2, steps)
 
     each(owners, cme, lambda o: abf_copy(o, cme).wait_recv())
     whole = ab_full[...].reshape(rows, LANES)
@@ -310,15 +323,19 @@
     cov_owners = min(cells_n, tiles)
     share = tiles // cov_owners
     dma = pltpu.SemaphoreType.DMA
+    anywhere = pl.BlockSpec(memory_space=pl.ANY)
     vmem = pl.BlockSpec(memory_space=pltpu.VMEM)
     packed = pl.pallas_call(
         functools.partial(
             kernel, groups, cells_n, float(rows * groups), float(cells * cells_n)
         ),
         out_shape=jax.ShapeDtypeStruct((slots, cells), F32),
-        in_specs=[pl.BlockSpec(memory_space=pl.ANY), vmem, vmem, vmem],
+        in_specs=[anywhere] * 4,
         out_specs=vmem,
         scratch_shapes=[
+            pltpu.VMEM((slots, blocks, rows), F32),
+            pltpu.VMEM((modes, cells), BF16),
+            pltpu.VMEM((1, count), jnp.int32),
             pltpu.VMEM((2, rows, half, cells), BF16),
             pltpu.VMEM((blocks, slots, rows), F32),
             pltpu.VMEM((2, cells, LANES), BF16),
@@ -332,14 +349,14 @@
             pltpu.VMEM((cells_n, share, 8, LANES), F32),
             pltpu.VMEM((cov_owners, share, 8, LANES), F32),
             pltpu.VMEM((groups, 2 * pairs, cells), F32),
-            dma((2, rows // STEP)),
+            dma((3,)), dma((2, rows // STEP)),
             dma((owners,)), dma((cells_n,)), dma((cells_n,)), dma((owners,)),
             dma((groups,)), dma((groups,)),
             dma((cov_owners,)), dma((cells_n,)), dma((cells_n,)), dma((cov_owners,)),
             dma((groups,)), dma((groups,)),
         ],
         compiler_params=pltpu.CompilerParams(
-            collective_id=0, has_side_effects=True, vmem_limit_bytes=40 * 2**20
+            collective_id=0, has_side_effects=True, vmem_limit_bytes=62 * 2**20
         ),
         cost_estimate=pl.CostEstimate(
             flops=2 * rows * slots * cells * modes, bytes_accessed=2 * rows * slots * cells,

time: 53.1 us -> 46.5 us (0.88)
  local copies, waits for them, and re-layouts: 7.09 us -> 2.92 us
  Pallas kernels: 45.1 us -> 42.7 us
    unnamed x9 -> x1, local copies, waits for them, and re-layouts: 6.49 us -> 1.57 us
    pallas_call x1, Pallas kernels: 45.1 us -> 42.7 us  [on_device(): pl.pallas_call(functools.partial(kernel, groups, cells_n, float(rows * gr...]
    slice x1, local copies, waits for them, and re-layouts: 0.6 us -> 1.36 us  [on_device(): return (packed[:count], packed[count])]
where the time goes in v2:
time: 46.5 us; the launch traced here: 46.3 us
  Pallas kernels  42.7 us (92%)
  local copies, waits for them, and re-layouts  2.92 us (6%)
  between operations  0.64 us (1%)
    pallas_call x1, Pallas kernels, on_device(): pl.pallas_call(functools.partial(kernel, groups, cells_n, float(rows * gr...  42.7 us
    unnamed x1, local copies, waits for them, and re-layouts  1.57 us
    slice x1, local copies, waits for them, and re-layouts, on_device(): return (packed[:count], packed[count])  1.36 us

profile of v2, /device:TPU:0, one launch (start us, length us, event | category | flops | bytes accessed | tf_op | source)
XLA Modules:
  0.0 46.3 jit_solution(11117251147942005150)
XLA Ops:
  0.6 42.7 %shard_map.59 = f32[32,1024]{1,0:T(8,128)} custom-call(bf16[128,32,1024]{2,1,0:T(8,128)(2,1)} %fields_ref.1, f32[32,8,128]{2,1,0:T(8,128)} %bitcast.6, bf16[64,1024]{1,0:T(8,128)(2,1)} %bitcast.7, s32[1,30]{1,0:T(1,128)} %bitcast.9), custom_call_target="tpu_custom_call" | custom-call | flops 536870912 | bytes 8388608 | tf_op jit(solution)/shard_map/pallas_call | solution.py:328
  43.4 1.4 %slice.7 = f32[1,1024]{1,0:T(1,128)} slice(f32[32,1024]{1,0:T(8,128)} %shard_map.59), slice={[30:31], [0:1024]} | slice | bytes 8192 | tf_op jit(solution)/shard_map/slice | solution.py:371
  44.7 1.6 %copy.7 = f32[30,1024]{1,0:T(8,128)} copy(f32[30,1024]{1,0:T(8,128)} %bitcast.5) | data formatting | bytes 245760

commit v3 on v2

--- a/solution.py
+++ b/solution.py
@@ -36,9 +36,9 @@
     fields_ref, scale_any, basis_any, order_any, out_ref,
     scale_ref, basis_ref, order_ref, field_buf, scale_buf, weight_buf, coef,
     ab_part, ab_recv, ab_full,
-    moment, grp_recv, quarter, cell_recv, cov_full, map_recv,
+    moment, pair_recv, grp_recv, quarter, cell_recv, cov_full, map_recv,
     input_sem, field_sem, ab_send, ab_sem, abf_send, abf_sem,
-    grp_send, grp_sem, cov_send, cov_sem, covf_send, covf_sem, map_send, map_sem,
+    pair_send, pair_sem, grp_send, grp_sem, cov_send, cov_sem, covf_send, covf_sem, map_send, map_sem,
 ):
     rows = field_buf.shape[1]
     half = field_buf.shape[2]
@@ -187,9 +187,20 @@
     own_square = own_square[:modes] + own_square[modes:]
     mode_lane = lax.broadcasted_iota(jnp.int32, (modes, LANES), 1)
 
+    core, rank = lax.rem(cme, 2), cme // 2
+    mine = pl.ds(core * quarter.shape[0], quarter.shape[0])
+    theirs = pl.ds((1 - core) * quarter.shape[0], quarter.shape[0])
+
+    def pair_copy(g):
+        return pltpu.make_async_remote_copy(
+            src_ref=moment.at[g, theirs], dst_ref=pair_recv.at[g],
+            send_sem=pair_send.at[g], recv_sem=pair_sem.at[g],
+            device_id={"cell": cme + 1 - 2 * core}, device_id_type=MESH,
+        )
+
     def grp_copy(target, source):
         return pltpu.make_async_remote_copy(
-            src_ref=moment.at[target], dst_ref=grp_recv.at[source],
+            src_ref=moment.at[target, mine], dst_ref=grp_recv.at[source],
             send_sem=grp_send.at[target], recv_sem=grp_sem.at[source],
             device_id={"grp": target}, device_id_type=MESH,
         )
@@ -213,24 +224,32 @@
                 at = (p + q) * tiles
                 moment[g, at:at + tiles] = matrix.reshape(tiles, 8, LANES)
 
+        pair_copy(g).start()
+
+    for g in range(groups):
+        pair_copy(g).wait_recv()
+        moment[g, mine] += pair_recv[g]
+
         @pl.when(g != gme)
         def _():
             grp_copy(g, gme).start()
 
-    grp_recv[gme] = moment[gme]
+    grp_recv[gme] = moment[gme, mine]
     each(groups, gme, lambda g: grp_copy(gme, g).wait_recv())
     total = grp_recv[0]
     for g in range(1, groups):
         total = total + grp_recv[g]
     quarter[...] = total
 
-    cov_owners, share = cov_full.shape[0], cov_full.shape[1]
+    cov_owners, share = cov_full.shape[0] // 2, cov_full.shape[1]
+    ranks = cells_n // 2
+    own = jnp.where(rank < cov_owners, core * cov_owners + rank, -1)
 
     def cov_copy(owner, source):
         return pltpu.make_async_remote_copy(
             src_ref=quarter.at[pl.ds(owner * share, share)], dst_ref=cell_recv.at[source],
             send_sem=cov_send.at[owner], recv_sem=cov_sem.at[source],
-            device_id={"cell": owner}, device_id_type=MESH,
+            device_id={"cell": 2 * owner + core}, device_id_type=MESH,
         )
 
     def covf_copy(owner, target):
@@ -240,17 +259,24 @@
             device_id={"cell": target}, device_id_type=MESH,
         )
 
-    each(cov_owners, cme, lambda o: cov_copy(o, cme).start())
-
-    @functools.partial(as_owner, cov_owners)
+    each(cov_owners, rank, lambda o: cov_copy(o, rank).start())
+
+    def as_cov_owner(body):
+        if cov_owners == ranks:
+            body()
+        else:
+            pl.when(rank < cov_owners)(body)
+
+    @as_cov_owner
     def _():
-        cov_full[cme] = quarter[pl.ds(cme * share, share)]
+        place = core * cov_owners + rank
+        cov_full[place] = quarter[pl.ds(rank * share, share)]
 
         def add(c):
-            cov_copy(cme, c).wait_recv()
-            cov_full[cme] += cell_recv[c]
-        each(cells_n, cme, add)
-        each(cells_n, cme, lambda c: covf_copy(cme, c).start())
+            cov_copy(rank, c).wait_recv()
+            cov_full[place] += cell_recv[c]
+        each(ranks, rank, add)
+        each(cells_n, cme, lambda c: covf_copy(place, c).start())
 
     slots = 2 * half
     count = order_ref.shape[1]
@@ -267,7 +293,7 @@
     select = jnp.concatenate([select] * 4, axis=1)
     basis_four = jnp.concatenate([phi_t] * 4, axis=0)
 
-    each(cov_owners, cme, lambda o: covf_copy(o, cme).wait_recv())
+    each(2 * cov_owners, own, lambda o: covf_copy(o, cme).wait_recv())
     pair_rows = cov_full[...].reshape(pairs * modes, LANES)
     matrices = [pair_rows[p * modes:(p + 1) * modes] * (1.0 / row_total) for p in range(pairs)]
     average = matrices[0] * 0.5
@@ -303,10 +329,14 @@
 
     each(owners, cme, lambda o: ab_copy(o, cme).wait_send())
     each(groups, gme, lambda g: grp_copy(g, gme).wait_send())
-    each(cov_owners, cme, lambda o: cov_copy(o, cme).wait_send())
+    each(cov_owners, rank, lambda o: cov_copy(o, rank).wait_send())
+    for g in range(groups):
+        pair_copy(g).wait_send()
     each(groups, gme, lambda g: map_copy(gme, g).wait_send())
     as_owner(owners, lambda: each(cells_n, cme, lambda c: abf_copy(cme, c).wait_send()))
-    as_owner(cov_owners, lambda: each(cells_n, cme, lambda c: covf_copy(cme, c).wait_send()))
+    as_cov_owner(lambda: each(
+        cells_n, cme, lambda c: covf_copy(core * cov_owners + rank, c).wait_send()
+    ))
 
 
 def on_device(fields, scales, pod_basis, param_order):
@@ -320,8 +350,9 @@
     count = param_order.shape[0]
     owners = min(cells_n, rows // 8)
     tiles = pairs * modes // 8
-    cov_owners = min(cells_n, tiles)
-    share = tiles // cov_owners
+    kept = tiles // 2
+    cov_owners = min(cells_n // 2, kept)
+    share = kept // cov_owners
     dma = pltpu.SemaphoreType.DMA
     anywhere = pl.BlockSpec(memory_space=pl.ANY)
     vmem = pl.BlockSpec(memory_space=pltpu.VMEM)
@@ -344,15 +375,16 @@
             pltpu.VMEM((cells_n, rows // owners, LANES), F32),
             pltpu.VMEM((owners, rows // owners, LANES), F32),
             pltpu.VMEM((groups, tiles, 8, LANES), F32),
-            pltpu.VMEM((groups, tiles, 8, LANES), F32),
-            pltpu.VMEM((tiles, 8, LANES), F32),
-            pltpu.VMEM((cells_n, share, 8, LANES), F32),
-            pltpu.VMEM((cov_owners, share, 8, LANES), F32),
+            pltpu.VMEM((groups, kept, 8, LANES), F32),
+            pltpu.VMEM((groups, kept, 8, LANES), F32),
+            pltpu.VMEM((kept, 8, LANES), F32),
+            pltpu.VMEM((cells_n // 2, share, 8, LANES), F32),
+            pltpu.VMEM((2 * cov_owners, share, 8, LANES), F32),
             pltpu.VMEM((groups, 2 * pairs, cells), F32),
             dma((3,)), dma((2, rows // STEP)),
             dma((owners,)), dma((cells_n,)), dma((cells_n,)), dma((owners,)),
-            dma((groups,)), dma((groups,)),
-            dma((cov_owners,)), dma((cells_n,)), dma((cells_n,)), dma((cov_owners,)),
+            dma((groups,)), dma((groups,)), dma((groups,)), dma((groups,)),
+            dma((cov_owners,)), dma((cells_n // 2,)), dma((cells_n,)), dma((2 * cov_owners,)),
             dma((groups,)), dma((groups,)),
         ],
         compiler_params=pltpu.CompilerParams(

time: 46.5 us -> 44 us (0.946)
  Pallas kernels: 42.7 us -> 40.2 us
    pallas_call x1, Pallas kernels: 42.7 us -> 40.2 us  [on_device(): pl.pallas_call(functools.partial(kernel, groups, cells_n, float(rows * gr...]
where the time goes in v3:
time: 44 us; the launch traced here: 43.8 us
  Pallas kernels  40.2 us (91%)
  local copies, waits for them, and re-layouts  2.92 us (7%)
  between operations  0.64 us (1%)
    pallas_call x1, Pallas kernels, on_device(): pl.pallas_call(functools.partial(kernel, groups, cells_n, float(rows * gr...  40.2 us
    unnamed x1, local copies, waits for them, and re-layouts  1.57 us
    slice x1, local copies, waits for them, and re-layouts, on_device(): return (packed[:count], packed[count])  1.36 us

profile of v3, /device:TPU:0, one launch (start us, length us, event | category | flops | bytes accessed | tf_op | source)
XLA Modules:
  0.0 43.8 jit_solution(16219122593315965643)
XLA Ops:
  0.6 40.2 %shard_map.59 = f32[32,1024]{1,0:T(8,128)} custom-call(bf16[128,32,1024]{2,1,0:T(8,128)(2,1)} %fields_ref.1, f32[32,8,128]{2,1,0:T(8,128)} %bitcast.6, bf16[64,1024]{1,0:T(8,128)(2,1)} %bitcast.7, s32[1,30]{1,0:T(1,128)} %bitcast.9), custom_call_target="tpu_custom_call" | custom-call | flops 536870912 | bytes 8388608 | tf_op jit(solution)/shard_map/pallas_call | solution.py:359
  40.8 1.4 %slice.7 = f32[1,1024]{1,0:T(1,128)} slice(f32[32,1024]{1,0:T(8,128)} %shard_map.59), slice={[30:31], [0:1024]} | slice | bytes 8192 | tf_op jit(solution)/shard_map/slice | solution.py:403
  42.2 1.6 %copy.7 = f32[30,1024]{1,0:T(8,128)} copy(f32[30,1024]{1,0:T(8,128)} %bitcast.5) | data formatting | bytes 245760
